TPU v7x, 32 devices: a whole 2x2x4 slice. The times are simulated.
32 devices in a mesh: dp: 8 (over z, x), tensor: 4 (over y, core).
Axes of the slice: x: 2, y: 2, z: 4, core: 2. Of those that a mesh axis runs over, the one named last changes fastest.
Arguments:
- hidden_in: bfloat16 [192, 4096], P('dp'), may hold values from -6 to 6
- queries: bfloat16 [192, 8192], P('dp', 'tensor'), may hold values from -150 to 150
- key_cache: bfloat16 [192, 4, 768, 128], P('dp', 'tensor'), may hold values from -5 to 5
- cached_value_rows: bfloat16 [192, 4, 768, 128], P('dp', 'tensor'), may hold values from -6 to 6
- cache_lengths: int32 [192], P('dp'), may hold values from 48 to 768, as said below
- out_weight: bfloat16 [8192, 4096], P('tensor', 'dp'), may hold values from -0.0625 to 0.0625
- expert_ids: int32 [192, 8], P('dp'), may hold values from 0 to 127, as said below
- route_probs: float32 [192, 8], P('dp'), may hold values from 0.05 to 1
- w_gate: bfloat16 [128, 4096, 768], P(('dp', 'tensor')), may hold values from -0.09375 to 0.09375
- w_up: bfloat16 [128, 4096, 768], P(('dp', 'tensor')), may hold values from -0.09375 to 0.09375
- w_down: bfloat16 [128, 768, 4096], P(('dp', 'tensor')), may hold values from -0.21875 to 0.21875
Outputs:
- layer_out: bfloat16 [192, 4096], P('dp', 'tensor')
Inputs may be any that keep to these rules, and one draw needn't show every extreme that they name: `expert_ids`: each row names 8 different experts; among the rows of one index of dp no expert is named more than 2 times, and one expert is named exactly 2 times in every such group of rows. Row r attends to cache positions 0 to cache_lengths[r] - 1; some row has all 768.
All inputs are finite; a program needn't handle non-finite values.
Results may differ from a plain program's by a relative error of at most 0.01.
Values may be sent and summed in bfloat16 or wider, within the bound.
A program may use at most 128 MiB of HBM per device.

v0:
```python
import math

import jax
import jax.numpy as jnp
from jax import lax
from jax.sharding import PartitionSpec as P

CAP = 2


def residual_norm(hidden_rows, projected):
    residual = (hidden_rows.astype(jnp.float32) + projected.astype(jnp.float32)).astype(
        jnp.bfloat16
    )
    resid_f = residual.astype(jnp.float32)
    normed = (
        resid_f * lax.rsqrt(jnp.mean(resid_f * resid_f, axis=-1, keepdims=True) + 1e-06)
    ).astype(jnp.bfloat16)
    return (residual, normed)


def local(
    hidden_in,
    queries,
    key_cache,
    cached_value_rows,
    cache_lengths,
    out_weight,
    expert_ids,
    route_probs,
    w_gate,
    w_up,
    w_down,
):
    dp_count = lax.axis_size("dp")
    tp_count = lax.axis_size("tensor")
    tp_rank = lax.axis_index("tensor")
    rows_dev, kv_local, cache_len, head_dim = key_cache.shape
    groups = queries.shape[1] // (kv_local * head_dim)
    model_width = hidden_in.shape[1]
    col_block = model_width // dp_count
    query_head_count = queries.reshape(rows_dev, kv_local, groups, head_dim)
    scores = jnp.einsum(
        "rhgd,rhld->rhgl", query_head_count, key_cache, preferred_element_type=jnp.float32
    ) * (1.0 / math.sqrt(head_dim))
    valid_mask = (jnp.arange(cache_len, dtype=jnp.int32)[None, :] < cache_lengths[:, None])[
        :, None, None, :
    ]
    scores = jnp.where(valid_mask, scores, -jnp.inf)
    largest = jnp.max(scores, axis=-1, keepdims=True)
    exponent = jnp.exp(scores - largest)
    attn_probs = (exponent / jnp.sum(exponent, axis=-1, keepdims=True)).astype(jnp.bfloat16)
    attn_out = jnp.einsum(
        "rhgl,rhld->rhgd", attn_probs, cached_value_rows, preferred_element_type=jnp.float32
    ).astype(jnp.bfloat16)
    attn_out = attn_out.reshape(rows_dev, kv_local * groups * head_dim)
    partial_value = jnp.dot(
        lax.all_gather(attn_out, "dp", axis=0, tiled=True),
        out_weight,
        preferred_element_type=jnp.float32,
    )
    partial_value = partial_value.reshape(dp_count, rows_dev, col_block)
    summed = lax.psum(partial_value.astype(jnp.bfloat16), "tensor")
    arrived = lax.all_to_all(summed, "dp", split_axis=0, concat_axis=2, tiled=True)
    residual, normed = residual_norm(hidden_in, arrived.reshape(rows_dev, model_width))
    exp_dev = w_gate.shape[0]
    owned = (
        (jnp.arange(dp_count, dtype=jnp.int32)[:, None] * tp_count + tp_rank) * exp_dev
        + jnp.arange(exp_dev, dtype=jnp.int32)[None, :]
    ).reshape(-1)
    matches = expert_ids[:, :, None] == owned[None, None, :]
    assigned = jnp.sum(matches.astype(jnp.int32), axis=1)
    slot_rank = jnp.cumsum(assigned, axis=0) - assigned
    slot_hit = (slot_rank[:, :, None] == jnp.arange(CAP, dtype=jnp.int32)[None, None, :]) & (
        assigned[:, :, None] > 0
    )
    route_weights = route_probs / jnp.sum(route_probs, axis=-1, keepdims=True)
    owned_weight = jnp.sum(jnp.where(matches, route_weights[:, :, None], 0.0), axis=1)
    outgoing = jnp.einsum(
        "rmc,rd->mcd", slot_hit.astype(jnp.bfloat16), normed, preferred_element_type=jnp.float32
    ).astype(jnp.bfloat16)
    outgoing = outgoing.reshape(dp_count, exp_dev, CAP, model_width)
    arrived_slots = lax.all_to_all(outgoing, "dp", split_axis=0, concat_axis=0, tiled=True)
    gate_proj = jnp.einsum(
        "sjcd,jdf->sjcf", arrived_slots, w_gate, preferred_element_type=jnp.float32
    )
    up_proj = jnp.einsum("sjcd,jdf->sjcf", arrived_slots, w_up, preferred_element_type=jnp.float32)
    activated = (jax.nn.silu(gate_proj) * up_proj).astype(jnp.bfloat16)
    expert_out = jnp.einsum(
        "sjcf,jfd->sjcd", activated, w_down, preferred_element_type=jnp.float32
    ).astype(jnp.bfloat16)
    results = lax.all_to_all(expert_out, "dp", split_axis=0, concat_axis=0, tiled=True)
    combine_table = jnp.where(slot_hit, owned_weight[:, :, None], 0.0)
    mixture = jnp.einsum(
        "rmc,mcd->rd",
        combine_table,
        results.reshape(dp_count * exp_dev, CAP, model_width).astype(jnp.float32),
        precision=lax.Precision.HIGHEST,
    )
    mixture_own = lax.psum_scatter(
        mixture.astype(jnp.bfloat16), "tensor", scatter_dimension=1, tiled=True
    ).astype(jnp.float32)
    width_share = model_width // tp_count
    residual_own = lax.dynamic_slice_in_dim(residual, tp_rank * width_share, width_share, 1)
    return (residual_own.astype(jnp.float32) + mixture_own).astype(jnp.bfloat16)


def solution(mesh):
    placed = (
        P("dp", None),
        P("dp", "tensor"),
        P("dp", "tensor", None, None),
        P("dp", "tensor", None, None),
        P("dp"),
        P("tensor", "dp"),
        P("dp", None),
        P("dp", None),
        P(("dp", "tensor"), None, None),
        P(("dp", "tensor"), None, None),
        P(("dp", "tensor"), None, None),
    )
    return jax.shard_map(
        local, mesh=mesh, in_specs=placed, out_specs=P("dp", "tensor"), check_vma=False
    )
```

profile of v0, /device:TPU:0, one launch (start us, length us, event | category | flops | bytes accessed | tf_op | source)
XLA Modules:
  0.0 190.4 jit_solution(8902086785829375313)
XLA Ops:
  6.5 1.1 copy.42
  7.6 0.7 iota_compare_fusion
  8.3 3.8 %fusion.63 = (f32[24,16]{1,0:T(8,128)S(1)}, f32[24,16,768]{2,1,0:T(8,128)S(1)}) fusion(bf16[24,16,128]{2,1,0:T(8,128)(2,1)S(1)} %bitcast.90, bf16[24,1,768,128]{3,2,1,0:T(8,128)(2,1)} %param.13, pred[24,768]{1,0:T(8,128)(4,1)S(1)} %iota_compare_fusion), kind=kOutput, calls=%fused_computation.61 | convolution fusion | flops 76677888 | bytes 6016512 | tf_op jit(solution)/shard_map/sub | solution.py:51
  12.2 3.1 %fusion.35 = bf16[24,16,128]{2,1,0:T(8,128)(2,1)S(1)} fusion(bf16[24,1,768,128]{3,2,1,0:T(8,128)(2,1)} %param.14, f32[24,16,768]{2,1,0:T(8,128)S(1)} %get-tuple-element.8, f32[24,16]{1,0:T(8,128)S(1)} %get-tuple-element.7), kind=kOutput, calls=%fused_computation.25 | convolution fusion | flops 76136448 | bytes 5998080 | tf_op jit(solution)/shard_map/rhgl,rhld->rhgd/dot_general | solution.py:53
  15.4 34.0 %all_gather.3 = bf16[192,2048]{1,0:T(8,128)(2,1)S(1)} all-gather(bf16[24,2048]{1,0:T(8,128)(2,1)S(1)} %bitcast.89), channel_id=1, replica_groups=mesh['dp'=8,'tensor'=4] {'dp'}, dimensions={0}, use_global_device_ids=true | all-gather | bytes 884736 | tf_op jit(solution)/shard_map/all_gather | solution.py:58
  49.3 1.3 convolution_convert_fusion.1
  50.6 32.8 %all-reduce.2.cloned.1.call-done = bf16[8,24,512]{2,1,0:T(8,128)(2,1)} async-done(((bf16[8,24,512]{2,1,0:T(8,128)(2,1)}), bf16[8,24,512]{2,1,0:T(8,128)(2,1)}) %all-reduce.2.cloned.1.call-update) | async-done | bytes 196624 | tf_op jit(solution)/shard_map/psum | solution.py:63
  83.4 5.5 %all-to-all-start = ((bf16[8,24,512]{2,1,0:T(8,128)(2,1)}), bf16[8,24,512]{2,1,0:T(8,128)(2,1)S(1)}, u32[]{:S(2)}, u32[]{:S(2)}) async-start(bf16[8,24,512]{2,1,0:T(8,128)(2,1)} %all-reduce.2.cloned.1.call-done), calls=%async_computation | async-start | bytes 393216 | tf_op jit(solution)/shard_map/all_to_all | solution.py:64
  89.2 0.1 fusion.50
  89.3 7.4 %all-to-all-done = bf16[8,24,512]{2,1,0:T(8,128)(2,1)S(1)} async-done(((bf16[8,24,512]{2,1,0:T(8,128)(2,1)}), bf16[8,24,512]{2,1,0:T(8,128)(2,1)S(1)}, u32[]{:S(2)}, u32[]{:S(2)}) %all-to-all-start) | async-done | bytes 196640 | tf_op jit(solution)/shard_map/all_to_all | solution.py:64
  96.8 0.2 fusion.45
  97.0 0.4 convolution_convert_fusion
  97.4 0.5 copy.41
  97.9 14.7 %all_to_all.19 = bf16[8,4,2,4096]{3,2,1,0:T(2,128)(2,1)S(1)} all-to-all(bf16[8,4,2,4096]{3,2,1,0:T(2,128)(2,1)S(1)} %bitcast.86), channel_id=1, replica_groups=mesh['dp'=8,'tensor'=4] {'dp'}, dimensions={0} | all-to-all | bytes 1048576 | tf_op jit(solution)/shard_map/all_to_all | solution.py:83
  112.6 9.9 %fusion.26 = f32[8,4,2,768]{3,0,2,1:T(8,128)S(1)} fusion(bf16[4,4096,768]{2,1,0:T(8,128)(2,1)} %param.19, bf16[8,4,2,4096]{3,2,1,0:T(2,128)(2,1)S(1)} %all_to_all.19), kind=kOutput, calls=%fused_computation.22 | convolution fusion | flops 402653184 | bytes 25886720 | tf_op jit(solution)/shard_map/sjcd,jdf->sjcf/dot_general | solution.py:84
  122.6 10.0 %fusion.38 = bf16[8,4,2,768]{3,0,2,1:T(8,128)(2,1)S(1)} fusion(bf16[4,4096,768]{2,1,0:T(8,128)(2,1)} %param.20, bf16[8,4,2,4096]{3,2,1,0:T(2,128)(2,1)S(1)} %all_to_all.19, f32[8,4,2,768]{3,0,2,1:T(8,128)S(1)} %fusion.26), kind=kOutput, calls=%fused_computation.26 | convolution fusion | flops 402948096 | bytes 25985024 | tf_op jit(solution)/shard_map/sjcd,jdf->sjcf/dot_general | solution.py:87
  132.6 11.7 %fusion.14 = bf16[8,4,2,4096]{3,0,2,1:T(8,128)(2,1)S(1)} fusion(bf16[8,4,2,768]{3,0,2,1:T(8,128)(2,1)S(1)} %fusion.38, bf16[4,768,4096]{2,1,0:T(8,128)(2,1)} %param.21), kind=kOutput, calls=%fused_computation.13 | convolution fusion | flops 402915328 | bytes 25788416 | tf_op jit(solution)/shard_map/sjcf,jfd->sjcd/dot_general | solution.py:89
  144.3 1.3 copy.36
  145.6 3.6 %all-to-all-start.2 = ((bf16[8,4,2,4096]{3,2,1,0:T(2,128)(2,1)}), bf16[8,4,2,4096]{3,2,1,0:T(2,128)(2,1)S(1)}, u32[]{:S(2)}, u32[]{:S(2)}) async-start(bf16[8,4,2,4096]{3,2,1,0:T(2,128)(2,1)} %copy.36), calls=%async_computation.2 | async-start | bytes 1048576 | tf_op jit(solution)/shard_map/all_to_all | solution.py:92
  149.4 0.1 fusion.51
  149.6 13.0 %all-to-all-done.2 = bf16[8,4,2,4096]{3,2,1,0:T(2,128)(2,1)S(1)} async-done(((bf16[8,4,2,4096]{3,2,1,0:T(2,128)(2,1)}), bf16[8,4,2,4096]{3,2,1,0:T(2,128)(2,1)S(1)}, u32[]{:S(2)}, u32[]{:S(2)}) %all-to-all-start.2) | async-done | bytes 524320 | tf_op jit(solution)/shard_map/all_to_all | solution.py:92
  162.5 1.3 fusion.17
  163.8 18.4 %reduce-scatter.2.cloned.1.call-done = bf16[24,1024]{1,0:T(8,128)(2,1)} async-done(((bf16[24,4096]{1,0:T(8,128)(2,1)}), bf16[24,1024]{1,0:T(8,128)(2,1)}) %reduce-scatter.2.cloned.1.call-update) | async-done | bytes 49168 | tf_op jit(solution)/shard_map/reduce_scatter | solution.py:100
  182.2 1.4 add_convert_fusion.1
  (28 shorter events, 0.6 us)
Async XLA Ops:
  6.5 42.8 %copy-start = (bf16[2048,512]{1,0:T(8,128)(2,1)S(1)}, bf16[2048,512]{1,0:T(8,128)(2,1)}, u32[]{:S(2)}) copy-start(bf16[2048,512]{1,0:T(8,128)(2,1)} %param.16) | copy-start | bytes 6291460
  6.5 76.9 %all-reduce.2.cloned.1.call-start = ((), (), s32[]{:S(2)}) async-start(), calls=%async_computation.4 | async-start | bytes 393216 | tf_op jit(solution)/shard_map/psum | solution.py:63
  12.2 76.9 %copy-start.4 = (s32[24,8]{0,1:T(8,128)S(1)}, s32[24,8]{0,1:T(8,128)}, u32[]{:S(2)}) copy-start(s32[24,8]{0,1:T(8,128)} %param.17) | copy-start | bytes 2308
  15.3 81.5 %copy-start.2 = (bf16[24,4096]{1,0:T(8,128)(2,1)S(1)}, bf16[24,4096]{1,0:T(8,128)(2,1)}, u32[]{:S(2)}) copy-start(bf16[24,4096]{1,0:T(8,128)(2,1)} %param.11) | copy-start | bytes 589828
  83.4 13.3 %all-to-all-start = ((bf16[8,24,512]{2,1,0:T(8,128)(2,1)}), bf16[8,24,512]{2,1,0:T(8,128)(2,1)S(1)}, u32[]{:S(2)}, u32[]{:S(2)}) async-start(bf16[8,24,512]{2,1,0:T(8,128)(2,1)} %all-reduce.2.cloned.1.call-done), calls=%async_computation | async-start | bytes 393216 | tf_op jit(solution)/shard_map/all_to_all | solution.py:64
  132.6 16.7 %copy-start.3 = (f32[24,8]{0,1:T(8,128)S(1)}, f32[24,8]{0,1:T(8,128)}, u32[]{:S(2)}) copy-start(f32[24,8]{0,1:T(8,128)} %param.18) | copy-start | bytes 2308
  132.6 51.0 %copy-start.1 = (bf16[2048,512]{1,0:T(8,128)(2,1)S(1)}, bf16[2048,512]{1,0:T(8,128)(2,1)}, u32[]{:S(2)}) copy-start(bf16[2048,512]{1,0:T(8,128)(2,1)} %param.16) | copy-start | bytes 6291460
  145.6 16.9 %all-to-all-start.2 = ((bf16[8,4,2,4096]{3,2,1,0:T(2,128)(2,1)}), bf16[8,4,2,4096]{3,2,1,0:T(2,128)(2,1)S(1)}, u32[]{:S(2)}, u32[]{:S(2)}) async-start(bf16[8,4,2,4096]{3,2,1,0:T(2,128)(2,1)} %copy.36), calls=%async_computation.2 | async-start | bytes 1048576 | tf_op jit(solution)/shard_map/all_to_all | solution.py:92
  149.3 32.9 %reduce-scatter.2.cloned.1.call-start = ((), (), s32[]{:S(2)}) async-start(), calls=%async_computation.5 | async-start | bytes 245760 | tf_op jit(solution)/shard_map/reduce_scatter | solution.py:100
Sparse Core Ops, SparseCore 0:
  50.7 32.6 all-reduce.1
  163.9 18.2 reduce-scatter.1
where the time goes:
time: 191 us; the launch traced here: 190 us
  waiting for transfers between devices  71.5 us (37%)
  blocking collectives  48.7 us (25%)
  matrix products  41.5 us (22%)
  between operations  13.5 us (7%)
  starting transfers between devices  9.18 us (5%)
  local copies, waits for them, and re-layouts  3.25 us (2%)
  other arithmetic  2.79 us (1%)
    all_gather x1, blocking collectives, local(): lax.all_gather(attn_out, 'dp', axis=0, tiled=True)  34 us
    psum x1, waiting for transfers between devices, local(): summed = lax.psum(partial_value.astype(jnp.bfloat16), 'tensor')  32.8 us
    reduce_scatter x1, waiting for transfers between devices, local(): lax.psum_scatter(mixture.astype(jnp.bfloat16), 'tensor', scatter_dimensio...  18.4 us
    all_to_all x1, blocking collectives, local(): lax.all_to_all(outgoing, 'dp', split_axis=0, concat_axis=0, tiled=True)  14.7 us
    all_to_all x1, waiting for transfers between devices, local(): lax.all_to_all(expert_out, 'dp', split_axis=0, concat_axis=0, tiled=True)  13 us
    dot_general x1, matrix products, local(): jnp.einsum('sjcf,jfd->sjcd', activated, w_down, preferred_element_type=jn...  11.7 us
    dot_general x1, matrix products, local(): jnp.einsum('sjcd,jdf->sjcf', arrived_slots, w_up, preferred_element_type=...  10 us
    dot_general x1, matrix products, local(): jnp.einsum('sjcd,jdf->sjcf', arrived_slots, w_gate, preferred_element_typ...  9.93 us
  transfers between devices with their start and end apart: 4, of which 4 were waited for; matrix products, arithmetic and copies ran while one was open for 0% of the time, Pallas kernels for 0%

commit v1 on v0

v1 whole, which is shorter than its diff:
```python
import functools
import math

import jax
import jax.numpy as jnp
from jax import lax
from jax.experimental import pallas as pl
from jax.experimental.pallas import tpu as pltpu
from jax.sharding import PartitionSpec as P

CAP = 2
SUB = 512
MESH = pl.DeviceIdType.MESH


def layer_kernel(
    G,
    T,
    E,
    R,
    attn_ref,
    hidden_ref,
    pick_ref,
    table_ref,
    wo_hbm,
    wg_hbm,
    wu_hbm,
    wd_hbm,
    out_ref,
    wo,
    wg,
    wu,
    wd,
    gathered,
    partial,
    rs_recv,
    summed,
    proj,
    residual,
    normed,
    outgoing,
    arrived,
    acc_g,
    acc_u,
    act,
    outs,
    results,
    wo_sem,
    wg_sem,
    wu_sem,
    wd_sem,
    s1,
    r1,
    s2,
    r2,
    s3,
    r3,
    s4,
    r4,
    s5,
    r5,
):
    d = lax.axis_index("dp")
    t = lax.axis_index("tensor")
    rows, width = hidden_ref.shape
    share = width // T
    cb = wo.shape[1]
    per = G // T
    ff = wg.shape[2]
    subs = share // SUB
    f32 = jnp.float32
    bf16 = jnp.bfloat16

    def remote(src, dst, ss, rs, dd, tt):
        return pltpu.make_async_remote_copy(
            src_ref=src,
            dst_ref=dst,
            send_sem=ss,
            recv_sem=rs,
            device_id=(dd, tt),
            device_id_type=MESH,
        )

    barrier = pltpu.get_barrier_semaphore()

    def greet(i, c):
        o = lax.rem(d * T + t + i, G * T)
        pl.semaphore_signal(barrier, inc=1, device_id=(o // T, lax.rem(o, T)), device_id_type=MESH)
        return c

    lax.fori_loop(1, G * T, greet, 0)

    wo_copy = pltpu.make_async_copy(wo_hbm, wo, wo_sem)
    wo_copy.start()

    def part(j):
        return pl.ds(j * share, share)

    def g_copy(j):
        return pltpu.make_async_copy(wg_hbm.at[:, part(j), :], wg.at[:, part(j), :], wg_sem.at[j])

    def u_copy(j):
        return pltpu.make_async_copy(wu_hbm.at[:, part(j), :], wu.at[:, part(j), :], wu_sem.at[j])

    def d_copy(s):
        j = lax.rem(t + 1 + s // subs, T)
        col = pl.multiple_of(j * share + (s % subs) * SUB, SUB)
        return pltpu.make_async_copy(
            wd_hbm.at[:, :, pl.ds(col, SUB)], wd.at[s % 2], wd_sem.at[s % 2]
        )

    pl.semaphore_wait(barrier, G * T - 1)

    def send1(i, c):
        p = lax.rem(d + i, G)
        remote(attn_ref, gathered.at[d], s1.at[p], r1.at[d], p, t).start()
        return c

    lax.fori_loop(1, G, send1, 0)
    for j in range(T):
        g_copy(j).start()
        u_copy(j).start()
    d_copy(0).start()
    d_copy(1).start()
    gathered[d] = attn_ref[...]
    wo_copy.wait()

    def project(i, c):
        g = lax.rem(d + G - i, G)

        @pl.when(i > 0)
        def _():
            remote(attn_ref, gathered.at[g], s1.at[g], r1.at[g], g, t).wait_recv()

        partial[g] = jnp.dot(gathered[g], wo[...], preferred_element_type=f32).astype(bf16)
        owner = g // per

        @pl.when(owner != t)
        def _():
            remote(
                partial.at[g], rs_recv.at[t, lax.rem(g, per)], s2.at[g], r2.at[t, lax.rem(g, per)], d, owner
            ).start()

        return c

    lax.fori_loop(0, G, project, 0)

    def reduce(k, c):
        g = t * per + k
        total = partial[g].astype(f32)
        for o in range(1, T):
            src = lax.rem(t + o, T)
            remote(partial.at[g], rs_recv.at[src, k], s2.at[g], r2.at[src, k], d, src).wait_recv()
            total = total + rs_recv[src, k].astype(f32)
        summed[k] = total.astype(bf16)
        for tt in range(T):
            own = jnp.logical_and(g == d, t == tt)

            @pl.when(own)
            def _():
                proj[d] = summed[k]

            @pl.when(jnp.logical_not(own))
            def _():
                remote(summed.at[k], proj.at[d], s3.at[k, tt], r3.at[d], g, tt).start()

        return c

    lax.fori_loop(0, per, reduce, 0)

    home = d // per

    def wait3(i, c):
        @pl.when(jnp.logical_not(jnp.logical_and(i == d, home == t)))
        def _():
            remote(summed.at[0], proj.at[i], s3.at[0, 0], r3.at[i], i, home).wait_recv()

        return c

    lax.fori_loop(0, G, wait3, 0)

    squares = jnp.zeros((rows, cb), f32)
    for g in range(G):
        cols = slice(g * cb, (g + 1) * cb)
        block = (hidden_ref[:, cols].astype(f32) + proj[g].astype(f32)).astype(bf16)
        residual[:, cols] = block
        bf = block.astype(f32)
        squares = squares + bf * bf
    scale = lax.rsqrt(jnp.sum(squares, axis=-1, keepdims=True) / width + 1e-06)
    for g in range(G):
        cols = slice(g * cb, (g + 1) * cb)
        normed[:, cols] = (residual[:, cols].astype(f32) * scale).astype(bf16)

    for j in range(T):
        block = jnp.dot(
            pick_ref[...], normed[:, j * share : (j + 1) * share], preferred_element_type=f32
        )
        outgoing[j] = block.reshape(G, R, share).astype(bf16)
        arrived[j, d] = outgoing[j, d]

        def send4(i, c, j=j):
            p = lax.rem(d + i, G)
            remote(outgoing.at[j, p], arrived.at[j, d], s4.at[j, p], r4.at[j, d], p, t).start()
            return c

        lax.fori_loop(1, G, send4, 0)

    for j in range(T):

        def wait4(i, c, j=j):
            p = lax.rem(d + G - i, G)
            remote(outgoing.at[j, p], arrived.at[j, p], s4.at[j, p], r4.at[j, p], p, t).wait_recv()
            return c

        lax.fori_loop(1, G, wait4, 0)
        g_copy(j).wait()
        u_copy(j).wait()

        def up(e, c, j=j):
            x = arrived[j].astype(f32).reshape(G * R, share).astype(bf16)
            gp = jnp.dot(x, wg[e, j * share : (j + 1) * share, :], preferred_element_type=f32)
            uq = jnp.dot(x, wu[e, j * share : (j + 1) * share, :], preferred_element_type=f32)
            if j == 0:
                acc_g[e] = gp
                acc_u[e] = uq
            else:
                gp = acc_g[e] + gp
                uq = acc_u[e] + uq
                if j < T - 1:
                    acc_g[e] = gp
                    acc_u[e] = uq
                else:
                    slot = lax.rem(lax.broadcasted_iota(jnp.int32, (G * R, ff), 0), R)
                    mine = (slot // CAP) == e
                    value = gp / (1.0 + jnp.exp(-gp)) * uq
                    act[e] = jnp.where(mine, value, 0.0).astype(bf16)
            return c

        lax.fori_loop(0, E, up, 0)

    for s in range(T * subs):
        d_copy(s).wait()
        half = s % subs
        total = jnp.dot(act[0], wd[s % 2, 0], preferred_element_type=f32)
        for e in range(1, E):
            total = total + jnp.dot(act[e], wd[s % 2, e], preferred_element_type=f32)
        n = s // subs
        outs[n, :, :, half * SUB : (half + 1) * SUB] = total.reshape(G, R, SUB).astype(bf16)
        if s + 2 < T * subs:
            d_copy(s + 2).start()
        if half == subs - 1:
            j = lax.rem(t + 1 + n, T)

            def send5(i, c, n=n, j=j):
                p = lax.rem(d + i, G)
                own = jnp.logical_and(p == d, j == t)

                @pl.when(own)
                def _():
                    results[d, t] = outs[n, p]

                @pl.when(jnp.logical_not(own))
                def _():
                    remote(
                        outs.at[n, p], results.at[d, t], s5.at[n, p], r5.at[d, t], p, j
                    ).start()

                return c

            lax.fori_loop(0, G, send5, 0)

    def wait5(i, c):
        o = lax.rem(d * T + t + i, G * T)
        p, q = o // T, lax.rem(o, T)
        remote(outs.at[0, p], results.at[p, q], s5.at[0, p], r5.at[p, q], p, q).wait_recv()
        return c

    lax.fori_loop(1, G * T, wait5, 0)
    back = results[...].astype(f32).reshape(G * T * R, share)
    mixture = jnp.dot(
        table_ref[...], back, precision=lax.Precision.HIGHEST, preferred_element_type=f32
    )
    mine = residual[:, pl.ds(pl.multiple_of(t * share, share), share)].astype(f32)
    out_ref[...] = (mine + mixture).astype(bf16)

    def drain1(i, c):
        p = lax.rem(d + i, G)
        remote(attn_ref, gathered.at[d], s1.at[p], r1.at[d], p, t).wait_send()
        for j in range(T):
            remote(outgoing.at[j, p], arrived.at[j, d], s4.at[j, p], r4.at[j, d], p, t).wait_send()
        return c

    lax.fori_loop(1, G, drain1, 0)

    def drain2(g, c):
        owner = g // per

        @pl.when(owner != t)
        def _():
            remote(partial.at[g], rs_recv.at[t, 0], s2.at[g], r2.at[t, 0], d, owner).wait_send()

        for n in range(T):
            j = lax.rem(t + 1 + n, T)

            @pl.when(jnp.logical_not(jnp.logical_and(g == d, j == t)))
            def _():
                remote(outs.at[n, g], results.at[d, t], s5.at[n, g], r5.at[d, t], g, j).wait_send()

        return c

    lax.fori_loop(0, G, drain2, 0)

    def drain3(k, c):
        g = t * per + k
        for tt in range(T):

            @pl.when(jnp.logical_not(jnp.logical_and(g == d, t == tt)))
            def _():
                remote(summed.at[k], proj.at[d], s3.at[k, tt], r3.at[d], g, tt).wait_send()

        return c

    lax.fori_loop(0, per, drain3, 0)


def local(
    hidden_in,
    queries,
    key_cache,
    cached_value_rows,
    cache_lengths,
    out_weight,
    expert_ids,
    route_probs,
    w_gate,
    w_up,
    w_down,
):
    G = lax.axis_size("dp")
    T = lax.axis_size("tensor")
    tp_rank = lax.axis_index("tensor")
    rows_dev, kv_local, cache_len, head_dim = key_cache.shape
    groups = queries.shape[1] // (kv_local * head_dim)
    width = hidden_in.shape[1]
    query_heads = queries.reshape(rows_dev, kv_local, groups, head_dim)
    scores = jnp.einsum(
        "rhgd,rhld->rhgl", query_heads, key_cache, preferred_element_type=jnp.float32
    ) * (1.0 / math.sqrt(head_dim))
    valid_mask = (jnp.arange(cache_len, dtype=jnp.int32)[None, :] < cache_lengths[:, None])[
        :, None, None, :
    ]
    scores = jnp.where(valid_mask, scores, -jnp.inf)
    largest = jnp.max(scores, axis=-1, keepdims=True)
    exponent = jnp.exp(scores - largest)
    attn_probs = (exponent / jnp.sum(exponent, axis=-1, keepdims=True)).astype(jnp.bfloat16)
    attn_out = jnp.einsum(
        "rhgl,rhld->rhgd", attn_probs, cached_value_rows, preferred_element_type=jnp.float32
    ).astype(jnp.bfloat16)
    attn_out = attn_out.reshape(rows_dev, kv_local * groups * head_dim)

    E, _, ff = w_gate.shape
    experts = G * T * E
    R = max(8, E * CAP)
    matches = expert_ids[:, :, None] == jnp.arange(experts, dtype=jnp.int32)[None, None, :]
    assigned = jnp.sum(matches.astype(jnp.int32), axis=1)
    slot_rank = jnp.cumsum(assigned, axis=0) - assigned
    slot_hit = (slot_rank[:, :, None] == jnp.arange(CAP, dtype=jnp.int32)[None, None, :]) & (
        assigned[:, :, None] > 0
    )
    route_weights = route_probs / jnp.sum(route_probs, axis=-1, keepdims=True)
    weight = jnp.sum(jnp.where(matches, route_weights[:, :, None], 0.0), axis=1)
    table = jnp.where(slot_hit, weight[:, :, None], 0.0).reshape(rows_dev, G * T, E * CAP)
    table = jnp.pad(table, ((0, 0), (0, 0), (0, R - E * CAP))).reshape(rows_dev, G * T * R)
    hit = slot_hit.astype(jnp.bfloat16).reshape(rows_dev, G, T, E * CAP)
    pick = lax.dynamic_index_in_dim(hit, tp_rank, 2, keepdims=False)
    pick = jnp.pad(pick, ((0, 0), (0, 0), (0, R - E * CAP))).reshape(rows_dev, G * R).T

    share = width // T
    hl = attn_out.shape[1]
    cb = out_weight.shape[1]
    per = G // T
    bf16 = jnp.bfloat16
    f32 = jnp.float32
    vmem = pl.BlockSpec(memory_space=pltpu.VMEM)
    hbm = pl.BlockSpec(memory_space=pl.ANY)
    dma = pltpu.SemaphoreType.DMA
    return pl.pallas_call(
        functools.partial(layer_kernel, G, T, E, R),
        out_shape=jax.ShapeDtypeStruct((rows_dev, share), bf16),
        in_specs=[vmem] * 4 + [hbm] * 4,
        out_specs=vmem,
        scratch_shapes=[
            pltpu.VMEM((hl, cb), bf16),
            pltpu.VMEM((E, width, ff), bf16),
            pltpu.VMEM((E, width, ff), bf16),
            pltpu.VMEM((2, E, ff, SUB), bf16),
            pltpu.VMEM((G, rows_dev, hl), bf16),
            pltpu.VMEM((G, rows_dev, cb), bf16),
            pltpu.VMEM((T, per, rows_dev, cb), bf16),
            pltpu.VMEM((per, rows_dev, cb), bf16),
            pltpu.VMEM((G, rows_dev, cb), bf16),
            pltpu.VMEM((rows_dev, width), bf16),
            pltpu.VMEM((rows_dev, width), bf16),
            pltpu.VMEM((T, G, R, share), bf16),
            pltpu.VMEM((T, G, R, share), bf16),
            pltpu.VMEM((E, G * R, ff), f32),
            pltpu.VMEM((E, G * R, ff), f32),
            pltpu.VMEM((E, G * R, ff), bf16),
            pltpu.VMEM((T, G, R, share), bf16),
            pltpu.VMEM((G, T, R, share), bf16),
            dma(()),
            dma((T,)),
            dma((T,)),
            dma((2,)),
            dma((G,)),
            dma((G,)),
            dma((G,)),
            dma((T, per)),
            dma((per, T)),
            dma((G,)),
            dma((T, G)),
            dma((T, G)),
            dma((T, G)),
            dma((G, T)),
        ],
        compiler_params=pltpu.CompilerParams(
            collective_id=0, has_side_effects=True, vmem_limit_bytes=66 * 1000 * 1000
        ),
    )(attn_out, hidden_in, pick, table, out_weight, w_gate, w_up, w_down)


def solution(mesh):
    placed = (
        P("dp", None),
        P("dp", "tensor"),
        P("dp", "tensor", None, None),
        P("dp", "tensor", None, None),
        P("dp"),
        P("tensor", "dp"),
        P("dp", None),
        P("dp", None),
        P(("dp", "tensor"), None, None),
        P(("dp", "tensor"), None, None),
        P(("dp", "tensor"), None, None),
    )
    return jax.shard_map(
        local, mesh=mesh, in_specs=placed, out_specs=P("dp", "tensor"), check_vma=False
    )
```

time: 191 us -> 89.8 us (0.47)
  Pallas kernels: 0 us -> 75.7 us
  waiting for transfers between devices: 71.5 us -> 0 us
  blocking collectives: 48.7 us -> 0 us
  matrix products: 41.5 us -> 7.02 us
  between operations: 13.5 us -> 0.11 us
  starting transfers between devices: 9.18 us -> 0 us
    pallas_call x0 -> x1, Pallas kernels: none -> 75.7 us  [local(): pl.pallas_call(functools.partial(layer_kernel, G, T, E, R), out_shape=jax...]
    dot_general x6 -> x0, matrix products: 34.5 us -> none  [the longest x1 11.7 us: local(): jnp.einsum('sjcf,jfd->sjcd', activated, w_down, preferred_element_type=jn...]
    all_gather x1 -> x0, blocking collectives: 34 us -> none  [local(): lax.all_gather(attn_out, 'dp', axis=0, tiled=True)]
    psum x1 -> x0, waiting for transfers between devices: 32.8 us -> none  [local(): summed = lax.psum(partial_value.astype(jnp.bfloat16), 'tensor')]
    all_to_all x2 -> x0, waiting for transfers between devices: 20.3 us -> none  [the longest x1 13 us: local(): lax.all_to_all(expert_out, 'dp', split_axis=0, concat_axis=0, tiled=True)]
    reduce_scatter x1 -> x0, waiting for transfers between devices: 18.4 us -> none  [local(): lax.psum_scatter(mixture.astype(jnp.bfloat16), 'tensor', scatter_dimensio...]
    all_to_all x1 -> x0, blocking collectives: 14.7 us -> none  [local(): lax.all_to_all(outgoing, 'dp', split_axis=0, concat_axis=0, tiled=True)]
    all_to_all x2 -> x0, starting transfers between devices: 9.15 us -> none  [the longest x1 5.51 us: local(): lax.all_to_all(summed, 'dp', split_axis=0, concat_axis=2, tiled=True)]
  transfers between devices with their start and end apart: 4 -> 0, of which waited for: 4 -> 0; matrix products, arithmetic and copies ran while one was open for 0% -> 0% of each run, Pallas kernels for 0% -> 0%
where the time goes in v1:
time: 89.8 us; the launch traced here: 89.4 us
  Pallas kernels  75.7 us (84%)
  matrix products  7.02 us (8%)
  local copies, waits for them, and re-layouts  4.24 us (5%)
  other arithmetic  2.35 us (3%)
    pallas_call x1, Pallas kernels, local(): pl.pallas_call(functools.partial(layer_kernel, G, T, E, R), out_shape=jax...  75.7 us
    sub x1, matrix products, local(): exponent = jnp.exp(scores - largest)  3.85 us
    dot_general x1, matrix products, local(): jnp.einsum('rhgl,rhld->rhgd', attn_probs, cached_value_rows, preferred_el...  3.17 us
    unnamed x8, local copies, waits for them, and re-layouts  3.07 us

profile of v1, /device:TPU:0, one launch (start us, length us, event | category | flops | bytes accessed | tf_op | source)
XLA Modules:
  0.0 89.4 jit_solution(9442918546650476666)
XLA Ops:
  0.0 0.9 %copy.31 = bf16[3,8,16,128]{3,2,1,0:T(8,128)(2,1)S(1)} copy(bf16[3,8,16,128]{3,1,2,0:T(8,128)(2,1)} %bitcast.37) | data formatting | bytes 196608
  0.9 0.7 iota_compare_fusion.1
  1.7 3.8 %fusion.20 = (f32[24,16]{1,0:T(8,128)S(1)}, f32[24,16,768]{2,1,0:T(8,128)S(1)}) fusion(bf16[24,16,128]{2,1,0:T(8,128)(2,1)S(1)} %bitcast.36, bf16[24,1,768,128]{3,2,1,0:T(8,128)(2,1)} %param.13, pred[24,768]{1,0:T(8,128)(4,1)S(1)} %iota_compare_fusion.1), kind=kOutput, calls=%fused_computation.24 | convolution fusion | flops 76677888 | bytes 6016512 | tf_op jit(solution)/shard_map/sub | solution.py:354
  5.5 3.2 %fusion.13 = bf16[24,16,128]{2,1,0:T(8,128)(2,1)S(1)} fusion(bf16[24,1,768,128]{3,2,1,0:T(8,128)(2,1)} %param.14, f32[24,16,768]{2,1,0:T(8,128)S(1)} %get-tuple-element.6, f32[24,16]{1,0:T(8,128)S(1)} %get-tuple-element.5), kind=kOutput, calls=%fused_computation.10 | convolution fusion | flops 76136448 | bytes 5998080 | tf_op jit(solution)/shard_map/rhgl,rhld->rhgd/dot_general | solution.py:356
  8.7 0.7 copy.34
  9.3 0.1 copy.23
  9.4 0.1 convert_reduce_fusion
  9.5 0.1 copy.25
  9.7 0.1 and.17
  9.7 0.1 and.18
  9.9 0.1 copy.24
  10.0 0.1 eq.50
  10.1 0.7 fusion.19.pick_ref
  10.8 0.1 copy.28
  10.9 0.1 select_reduce_fusion
  11.0 0.1 copy.29
  11.2 0.1 copy.30
  11.3 0.1 and.20
  11.4 0.1 copy.27
  11.4 0.1 copy.26
  11.5 0.1 eq.55
  11.7 0.6 and_select_fusion.table_ref
  12.3 75.7 %shard_map.109 = bf16[24,1024]{1,0:T(8,128)(2,1)} custom-call(bf16[24,2048]{1,0:T(8,128)(2,1)} %bitcast.35, bf16[24,4096]{1,0:T(8,128)(2,1)} %hidden_ref.1, bf16[64,24]{1,0:T(8,128)(2,1)} %fusion.19.pick_ref, f32[24,256]{1,0:T(8,128)} %and_select_fusion.table_ref, bf16[2048,512]{1,0:T(8,128)(2,1)} %wo_hbm.1, bf16[4,4096,768]{2,1,0:T(8,128)(2,1)} %wg_hbm.1, ...), custom_call_target="tpu_custom_call" | custom-call | tf_op jit(solution)/shard_map/pallas_call | solution.py:387
  88.0 1.4 %copy.36 = bf16[24,1024]{1,0:T(8,128)(2,1)} copy(bf16[24,1024]{1,0:T(8,128)(2,1)} %shard_map.109) | data formatting | bytes 98304
  (13 shorter events, 0.2 us)
Async XLA Ops:
  5.5 3.8 %copy-start.1 = (s32[24,8]{0,1:T(8,128)S(1)}, s32[24,8]{0,1:T(8,128)}, u32[]{:S(2)}) copy-start(s32[24,8]{0,1:T(8,128)} %param.17) | copy-start | bytes 2308
  5.5 5.3 %copy-start = (f32[24,8]{0,1:T(8,128)S(1)}, f32[24,8]{0,1:T(8,128)}, u32[]{:S(2)}) copy-start(f32[24,8]{0,1:T(8,128)} %param.18) | copy-start | bytes 2308

commit v2 on v1

--- a/solution.py
+++ b/solution.py
@@ -10,6 +10,7 @@
 
 CAP = 2
 SUB = 512
+INNER = 2
 MESH = pl.DeviceIdType.MESH
 
 
@@ -20,8 +21,8 @@
     R,
     attn_ref,
     hidden_ref,
-    pick_ref,
-    table_ref,
+    ids_ref,
+    probs_ref,
     wo_hbm,
     wg_hbm,
     wu_hbm,
@@ -45,12 +46,15 @@
     act,
     outs,
     results,
+    pick,
+    table,
     wo_sem,
     wg_sem,
     wu_sem,
     wd_sem,
     s1,
     r1,
+    sf,
     s2,
     r2,
     s3,
@@ -105,32 +109,85 @@
     def d_copy(s):
         j = lax.rem(t + 1 + s // subs, T)
         col = pl.multiple_of(j * share + (s % subs) * SUB, SUB)
-        return pltpu.make_async_copy(
-            wd_hbm.at[:, :, pl.ds(col, SUB)], wd.at[s % 2], wd_sem.at[s % 2]
-        )
+        return pltpu.make_async_copy(wd_hbm.at[:, :, pl.ds(col, SUB)], down_at(s), wd_sem.at[s])
+
+    def down_at(s):
+        if s < 2:
+            return wd.at[s]
+        k = (s - 2) // 2
+        return (wg, wu)[s % 2].at[:, k * share : k * share + ff, 0:SUB]
+
+    subs_all = T * subs
 
     pl.semaphore_wait(barrier, G * T - 1)
 
+    outer = G // INNER
+    inner = lax.rem(d, INNER)
+    mate = d + 1 - 2 * inner
+
+    def far(i):
+        return lax.rem(d + INNER * i, G)
+
+    def first(p):
+        return remote(attn_ref, gathered.at[d], s1.at[p], r1.at[d], p, t)
+
+    first(mate).start()
+
     def send1(i, c):
-        p = lax.rem(d + i, G)
-        remote(attn_ref, gathered.at[d], s1.at[p], r1.at[d], p, t).start()
-        return c
-
-    lax.fori_loop(1, G, send1, 0)
+        first(far(i)).start()
+        return c
+
+    lax.fori_loop(1, outer, send1, 0)
     for j in range(T):
         g_copy(j).start()
         u_copy(j).start()
     d_copy(0).start()
     d_copy(1).start()
     gathered[d] = attn_ref[...]
+
+    ids = ids_ref[...]
+    probs = probs_ref[...]
+    shares = probs / jnp.sum(probs, axis=-1, keepdims=True)
+    below = lax.broadcasted_iota(jnp.int32, (rows, rows), 0) > lax.broadcasted_iota(
+        jnp.int32, (rows, rows), 1
+    )
+    below = jnp.where(below, 1.0, 0.0).astype(bf16)
+
+    def routes(count, device_of):
+        col = lax.broadcasted_iota(jnp.int32, (rows, count), 1)
+        place = lax.rem(col, R)
+        expert = device_of(lax.div(col, R)) * E + lax.div(place, CAP)
+        slot = lax.rem(place, CAP)
+        assigned = jnp.zeros((rows, count), f32)
+        weight = jnp.zeros((rows, count), f32)
+        for k in range(ids.shape[1]):
+            same = ids[:, k : k + 1] == expert
+            assigned = assigned + jnp.where(same, 1.0, 0.0)
+            weight = weight + jnp.where(same, shares[:, k : k + 1], 0.0)
+        rank = jnp.dot(below, assigned.astype(bf16), preferred_element_type=f32)
+        hit = (assigned > 0.5) & (rank.astype(jnp.int32) == slot) & (place < E * CAP)
+        return hit, weight
+
+    hit, weight = routes(G * T * R, lambda n: n)
+    table[...] = jnp.where(hit, weight, 0.0)
+    hit, weight = routes(G * R, lambda n: n * T + t)
+    pick[...] = jnp.where(hit, 1.0, 0.0).astype(bf16)
     wo_copy.wait()
 
     def project(i, c):
-        g = lax.rem(d + G - i, G)
+        near = i < outer + 1
+        k = jnp.where(near, i - 1, i - outer)
+        base = lax.rem(d + G - INNER * k, G)
+        straight = jnp.logical_and(i > 1, near)
+        g = jnp.where(i == 0, d, jnp.where(straight, base, base + 1 - 2 * inner))
 
         @pl.when(i > 0)
         def _():
             remote(attn_ref, gathered.at[g], s1.at[g], r1.at[g], g, t).wait_recv()
+
+        @pl.when(straight)
+        def _():
+            remote(gathered.at[g], gathered.at[g], sf.at[g], r1.at[g], mate, t).start()
 
         partial[g] = jnp.dot(gathered[g], wo[...], preferred_element_type=f32).astype(bf16)
         owner = g // per
@@ -192,8 +249,11 @@
         normed[:, cols] = (residual[:, cols].astype(f32) * scale).astype(bf16)
 
     for j in range(T):
-        block = jnp.dot(
-            pick_ref[...], normed[:, j * share : (j + 1) * share], preferred_element_type=f32
+        block = lax.dot_general(
+            pick[...],
+            normed[:, j * share : (j + 1) * share],
+            (((0,), (0,)), ((), ())),
+            preferred_element_type=f32,
         )
         outgoing[j] = block.reshape(G, R, share).astype(bf16)
         arrived[j, d] = outgoing[j, d]
@@ -237,17 +297,19 @@
             return c
 
         lax.fori_loop(0, E, up, 0)
+        for s in (2 * j + 2, 2 * j + 3):
+            if s < subs_all:
+                d_copy(s).start()
 
     for s in range(T * subs):
         d_copy(s).wait()
         half = s % subs
-        total = jnp.dot(act[0], wd[s % 2, 0], preferred_element_type=f32)
+        down = down_at(s)
+        total = jnp.dot(act[0], down[0], preferred_element_type=f32)
         for e in range(1, E):
-            total = total + jnp.dot(act[e], wd[s % 2, e], preferred_element_type=f32)
+            total = total + jnp.dot(act[e], down[e], preferred_element_type=f32)
         n = s // subs
         outs[n, :, :, half * SUB : (half + 1) * SUB] = total.reshape(G, R, SUB).astype(bf16)
-        if s + 2 < T * subs:
-            d_copy(s + 2).start()
         if half == subs - 1:
             j = lax.rem(t + 1 + n, T)
 
@@ -278,19 +340,27 @@
     lax.fori_loop(1, G * T, wait5, 0)
     back = results[...].astype(f32).reshape(G * T * R, share)
     mixture = jnp.dot(
-        table_ref[...], back, precision=lax.Precision.HIGHEST, preferred_element_type=f32
+        table[...], back, precision=lax.Precision.HIGHEST, preferred_element_type=f32
     )
     mine = residual[:, pl.ds(pl.multiple_of(t * share, share), share)].astype(f32)
     out_ref[...] = (mine + mixture).astype(bf16)
 
     def drain1(i, c):
         p = lax.rem(d + i, G)
-        remote(attn_ref, gathered.at[d], s1.at[p], r1.at[d], p, t).wait_send()
         for j in range(T):
             remote(outgoing.at[j, p], arrived.at[j, d], s4.at[j, p], r4.at[j, d], p, t).wait_send()
         return c
 
     lax.fori_loop(1, G, drain1, 0)
+    first(mate).wait_send()
+
+    def drain0(i, c):
+        first(far(i)).wait_send()
+        g = far(i)
+        remote(gathered.at[g], gathered.at[g], sf.at[g], r1.at[g], mate, t).wait_send()
+        return c
+
+    lax.fori_loop(1, outer, drain0, 0)
 
     def drain2(g, c):
         owner = g // per
@@ -359,22 +429,7 @@
     attn_out = attn_out.reshape(rows_dev, kv_local * groups * head_dim)
 
     E, _, ff = w_gate.shape
-    experts = G * T * E
     R = max(8, E * CAP)
-    matches = expert_ids[:, :, None] == jnp.arange(experts, dtype=jnp.int32)[None, None, :]
-    assigned = jnp.sum(matches.astype(jnp.int32), axis=1)
-    slot_rank = jnp.cumsum(assigned, axis=0) - assigned
-    slot_hit = (slot_rank[:, :, None] == jnp.arange(CAP, dtype=jnp.int32)[None, None, :]) & (
-        assigned[:, :, None] > 0
-    )
-    route_weights = route_probs / jnp.sum(route_probs, axis=-1, keepdims=True)
-    weight = jnp.sum(jnp.where(matches, route_weights[:, :, None], 0.0), axis=1)
-    table = jnp.where(slot_hit, weight[:, :, None], 0.0).reshape(rows_dev, G * T, E * CAP)
-    table = jnp.pad(table, ((0, 0), (0, 0), (0, R - E * CAP))).reshape(rows_dev, G * T * R)
-    hit = slot_hit.astype(jnp.bfloat16).reshape(rows_dev, G, T, E * CAP)
-    pick = lax.dynamic_index_in_dim(hit, tp_rank, 2, keepdims=False)
-    pick = jnp.pad(pick, ((0, 0), (0, 0), (0, R - E * CAP))).reshape(rows_dev, G * R).T
-
     share = width // T
     hl = attn_out.shape[1]
     cb = out_weight.shape[1]
@@ -408,10 +463,13 @@
             pltpu.VMEM((E, G * R, ff), bf16),
             pltpu.VMEM((T, G, R, share), bf16),
             pltpu.VMEM((G, T, R, share), bf16),
+            pltpu.VMEM((rows_dev, G * R), bf16),
+            pltpu.VMEM((rows_dev, G * T * R), f32),
             dma(()),
             dma((T,)),
             dma((T,)),
-            dma((2,)),
+            dma((T * (share // SUB),)),
+            dma((G,)),
             dma((G,)),
             dma((G,)),
             dma((G,)),
@@ -426,7 +484,7 @@
         compiler_params=pltpu.CompilerParams(
             collective_id=0, has_side_effects=True, vmem_limit_bytes=66 * 1000 * 1000
         ),
-    )(attn_out, hidden_in, pick, table, out_weight, w_gate, w_up, w_down)
+    )(attn_out, hidden_in, expert_ids, route_probs, out_weight, w_gate, w_up, w_down)
 
 
 def solution(mesh):

time: 89.8 us -> 81.1 us (0.903)
  Pallas kernels: 75.7 us -> 68.7 us
  other arithmetic: 2.35 us -> 0.74 us
    pallas_call x1, Pallas kernels: 75.7 us -> 68.7 us  [local(): pl.pallas_call(functools.partial(layer_kernel, G, T, E, R), out_shape=jax...]
    unnamed x8 -> x9, local copies, waits for them, and re-layouts: 3.07 us -> 4.33 us
where the time goes in v2:
time: 81.1 us; the launch traced here: 80.8 us
  Pallas kernels  68.7 us (85%)
  matrix products  7.02 us (9%)
  local copies, waits for them, and re-layouts  4.33 us (5%)
    pallas_call x1, Pallas kernels, local(): pl.pallas_call(functools.partial(layer_kernel, G, T, E, R), out_shape=jax...  68.7 us
    unnamed x9, local copies, waits for them, and re-layouts  4.33 us
    sub x1, matrix products, local(): exponent = jnp.exp(scores - largest)  3.85 us
    dot_general x1, matrix products, local(): jnp.einsum('rhgl,rhld->rhgd', attn_probs, cached_value_rows, preferred_el...  3.17 us

profile of v2, /device:TPU:0, one launch (start us, length us, event | category | flops | bytes accessed | tf_op | source)
XLA Modules:
  0.0 80.8 jit_solution(5928291453806599516)
XLA Ops:
  0.0 0.9 %copy.14 = bf16[3,8,16,128]{3,2,1,0:T(8,128)(2,1)S(1)} copy(bf16[3,8,16,128]{3,1,2,0:T(8,128)(2,1)} %bitcast.23) | data formatting | bytes 196608
  0.9 0.7 iota_compare_fusion
  1.7 3.8 %fusion.17 = (f32[24,16]{1,0:T(8,128)S(1)}, f32[24,16,768]{2,1,0:T(8,128)S(1)}) fusion(bf16[24,16,128]{2,1,0:T(8,128)(2,1)S(1)} %bitcast.21, bf16[24,1,768,128]{3,2,1,0:T(8,128)(2,1)} %param.13, pred[24,768]{1,0:T(8,128)(4,1)S(1)} %iota_compare_fusion), kind=kOutput, calls=%fused_computation.14 | convolution fusion | flops 76677888 | bytes 6016512 | tf_op jit(solution)/shard_map/sub | solution.py:424
  5.5 0.0 copy-start
  5.5 0.0 copy-start.1
  5.5 3.2 %fusion.13 = bf16[24,16,128]{2,1,0:T(8,128)(2,1)S(1)} fusion(bf16[24,1,768,128]{3,2,1,0:T(8,128)(2,1)} %param.14, f32[24,16,768]{2,1,0:T(8,128)S(1)} %get-tuple-element.6, f32[24,16]{1,0:T(8,128)S(1)} %get-tuple-element.5), kind=kOutput, calls=%fused_computation.10 | convolution fusion | flops 76136448 | bytes 5998080 | tf_op jit(solution)/shard_map/rhgl,rhld->rhgd/dot_general | solution.py:426
  8.7 0.7 copy.17
  9.3 0.0 copy-done
  9.3 0.7 copy.12.ids_ref
  10.0 0.0 copy-done.1
  10.0 0.7 copy.13.probs_ref
  10.7 68.7 %shard_map.109 = bf16[24,1024]{1,0:T(8,128)(2,1)} custom-call(bf16[24,2048]{1,0:T(8,128)(2,1)} %bitcast.22, bf16[24,4096]{1,0:T(8,128)(2,1)} %hidden_ref.1, s32[24,8]{1,0:T(8,128)} %copy.12.ids_ref, f32[24,8]{1,0:T(8,128)} %copy.13.probs_ref, bf16[2048,512]{1,0:T(8,128)(2,1)} %wo_hbm.1, bf16[4,4096,768]{2,1,0:T(8,128)(2,1)} %wg_hbm.1, ...), custom_call_target="tpu_custom_call" | custom-call | tf_op jit(solution)/shard_map/pallas_call | solution.py:442
  79.4 1.4 %copy.19 = bf16[24,1024]{1,0:T(8,128)(2,1)} copy(bf16[24,1024]{1,0:T(8,128)(2,1)} %shard_map.109) | data formatting | bytes 98304
Async XLA Ops:
  5.5 3.8 %copy-start = (s32[24,8]{0,1:T(8,128)S(1)}, s32[24,8]{0,1:T(8,128)}, u32[]{:S(2)}) copy-start(s32[24,8]{0,1:T(8,128)} %param.17) | copy-start | bytes 2308
  5.5 4.5 %copy-start.1 = (f32[24,8]{0,1:T(8,128)S(1)}, f32[24,8]{0,1:T(8,128)}, u32[]{:S(2)}) copy-start(f32[24,8]{0,1:T(8,128)} %param.18) | copy-start | bytes 2308

commit v3 on v2

--- a/solution.py
+++ b/solution.py
@@ -138,15 +138,15 @@
         return c
 
     lax.fori_loop(1, outer, send1, 0)
-    for j in range(T):
+    def fetch(j):
         g_copy(j).start()
         u_copy(j).start()
-    d_copy(0).start()
-    d_copy(1).start()
+
+    fetch(0)
     gathered[d] = attn_ref[...]
 
-    ids = ids_ref[...]
-    probs = probs_ref[...]
+    ids = ids_ref[...].T
+    probs = probs_ref[...].T
     shares = probs / jnp.sum(probs, axis=-1, keepdims=True)
     below = lax.broadcasted_iota(jnp.int32, (rows, rows), 0) > lax.broadcasted_iota(
         jnp.int32, (rows, rows), 1
@@ -189,6 +189,10 @@
         def _():
             remote(gathered.at[g], gathered.at[g], sf.at[g], r1.at[g], mate, t).start()
 
+        @pl.when(i == outer)
+        def _():
+            fetch(1)
+
         partial[g] = jnp.dot(gathered[g], wo[...], preferred_element_type=f32).astype(bf16)
         owner = g // per
 
@@ -201,6 +205,8 @@
         return c
 
     lax.fori_loop(0, G, project, 0)
+    for j in range(2, T - 1):
+        fetch(j)
 
     def reduce(k, c):
         g = t * per + k
@@ -225,6 +231,7 @@
 
     lax.fori_loop(0, per, reduce, 0)
 
+    fetch(T - 1)
     home = d // per
 
     def wait3(i, c):
@@ -235,6 +242,9 @@
         return c
 
     lax.fori_loop(0, G, wait3, 0)
+
+    d_copy(0).start()
+    d_copy(1).start()
 
     squares = jnp.zeros((rows, cb), f32)
     for g in range(G):
@@ -484,7 +494,7 @@
         compiler_params=pltpu.CompilerParams(
             collective_id=0, has_side_effects=True, vmem_limit_bytes=66 * 1000 * 1000
         ),
-    )(attn_out, hidden_in, expert_ids, route_probs, out_weight, w_gate, w_up, w_down)
+    )(attn_out, hidden_in, expert_ids.T, route_probs.T, out_weight, w_gate, w_up, w_down)
 
 
 def solution(mesh):

time: 81.1 us -> 79.8 us (0.984)
  local copies, waits for them, and re-layouts: 4.33 us -> 2.99 us
    unnamed x9 -> x3, local copies, waits for them, and re-layouts: 4.33 us -> 2.99 us
where the time goes in v3:
time: 79.8 us; the launch traced here: 79.4 us
  Pallas kernels  68.7 us (86%)
  matrix products  6.97 us (9%)
  local copies, waits for them, and re-layouts  2.99 us (4%)
    pallas_call x1, Pallas kernels, local(): pl.pallas_call(functools.partial(layer_kernel, G, T, E, R), out_shape=jax...  68.7 us
    sub x1, matrix products, local(): exponent = jnp.exp(scores - largest)  3.84 us
    dot_general x1, matrix products, local(): jnp.einsum('rhgl,rhld->rhgd', attn_probs, cached_value_rows, preferred_el...  3.13 us
    unnamed x3, local copies, waits for them, and re-layouts  2.99 us

profile of v3, /device:TPU:0, one launch (start us, length us, event | category | flops | bytes accessed | tf_op | source)
XLA Modules:
  0.0 79.4 jit_solution(9469034993982037028)
XLA Ops:
  0.0 0.7 iota_compare_fusion
  0.7 0.9 %copy.12 = bf16[3,8,16,128]{3,2,1,0:T(8,128)(2,1)S(1)} copy(bf16[3,8,16,128]{3,1,2,0:T(8,128)(2,1)} %bitcast.25) | data formatting | bytes 196608
  1.7 3.8 %fusion.17 = (f32[24,16]{1,0:T(8,128)S(1)}, f32[24,16,768]{2,1,0:T(8,128)S(1)}) fusion(bf16[24,16,128]{2,1,0:T(8,128)(2,1)S(1)} %bitcast.24, bf16[24,1,768,128]{3,2,1,0:T(8,128)(2,1)} %param.13, pred[24,768]{1,0:T(8,128)(4,1)S(1)} %iota_compare_fusion), kind=kOutput, calls=%fused_computation.14 | convolution fusion | flops 76677888 | bytes 6016512 | tf_op jit(solution)/shard_map/sub | solution.py:434
  5.5 3.1 %fusion.13 = bf16[24,16,128]{2,1,0:T(8,128)(2,1)S(1)} fusion(bf16[24,1,768,128]{3,2,1,0:T(8,128)(2,1)} %param.14, f32[24,16,768]{2,1,0:T(8,128)S(1)} %get-tuple-element.6, f32[24,16]{1,0:T(8,128)S(1)} %get-tuple-element.5), kind=kOutput, calls=%fused_computation.10 | convolution fusion | flops 76136448 | bytes 5998080 | tf_op jit(solution)/shard_map/rhgl,rhld->rhgd/dot_general | solution.py:436
  8.6 0.7 copy.15
  9.3 68.7 %shard_map.109 = bf16[24,1024]{1,0:T(8,128)(2,1)} custom-call(bf16[24,2048]{1,0:T(8,128)(2,1)} %bitcast.23, bf16[24,4096]{1,0:T(8,128)(2,1)} %hidden_ref.1, s32[8,24]{1,0:T(8,128)} %bitcast.27, f32[8,24]{1,0:T(8,128)} %bitcast.28, bf16[2048,512]{1,0:T(8,128)(2,1)} %wo_hbm.1, bf16[4,4096,768]{2,1,0:T(8,128)(2,1)} %wg_hbm.1, bf16[4,4096,768]{2,1,0:T(8,128)(2,1)} %wu_hbm.1, ...), custom_call_target="tpu_custom_call" | custom-call | tf_op jit(solution)/shard_map/pallas_call | solution.py:452
  78.0 1.4 %copy.17 = bf16[24,1024]{1,0:T(8,128)(2,1)} copy(bf16[24,1024]{1,0:T(8,128)(2,1)} %shard_map.109) | data formatting | bytes 98304
